TPU v7x, 32 devices: a whole 2x2x4 slice. The times are simulated.
32 devices in a mesh: dp: 16 (over z, x, core), mp: 2 (over y).
Axes of the slice: x: 2, y: 2, z: 4, core: 2. Of those that a mesh axis runs over, the one named last changes fastest.
Arguments:
- tokens: float32 [16384, 768], P('dp'), may hold values from -6 to 6
- conditioning: float32 [64, 768], P('dp'), may hold values from -5 to 5
- sigmas: float32 [64], P('dp'), may hold values from 0.07 to 3.3
- positions: int32 [64, 2, 256], P('dp'), may hold values from 0 to 15, as said below
- cotangent: bfloat16 [16384, 768], P('dp'), may hold values from -6 to 6
- owners: int32 [2, 180], P('mp'), may hold values from 0 to 15, as said below
- master: float32 [2, 192, 32, 768], P('mp', 'dp'), may hold values from -0.57735027 to 0.57735027, as said below
- moment_one: float32 [2, 192, 32, 768], P('mp', 'dp'), may hold values from -256 to 256, as said below
- moment_two: float32 [2, 192, 32, 768], P('mp', 'dp'), may hold values from 0 to 16384, as said below
- scale_state: float32 [3, 12], P(None, 'mp'), may hold values from -153.6 to 5898.24, as said below
Outputs:
- output: float32 [16384, 768], P('dp')
- input_grad: float32 [16384, 768], P('dp')
- weight_grads: float32 [2, 180, 24576], P('mp', None, 'dp')
- new_master: float32 [2, 192, 32, 768], P('mp', 'dp')
- new_moment_one: float32 [2, 192, 32, 768], P('mp', 'dp')
- new_moment_two: float32 [2, 192, 32, 768], P('mp', 'dp')
- scale_update: float32 [2, 12], P(None, 'mp')
- scale_moment_two: float32 [12], P('mp')
Inputs may be any that keep to these rules, and one draw needn't show every extreme that they name: owners[h, u] is the index of dp whose slots hold unit u of half h; no index holds more than 12 units of one half, and in each half some index holds exactly 12. `positions`: each image's (row, column) pairs visit every cell of the 16 x 16 grid once. `master`: slots that no unit fills are zero. `moment_one`: slots that no unit fills are zero. `moment_two`: slots that no unit fills are zero; the others are positive. `scale_state`: row 0 lies between 6 and 14, row 2 is positive.
All inputs are finite; a program needn't handle non-finite values.
Results may differ from a plain program's by a relative error of at most 0.024.
Values may be sent and summed in bfloat16 or wider, within the bound.
No kernel may reach another device: no remote copies, remote signals or barrier semaphores. Data moves between devices by JAX's collectives and lax.ppermute only.
A program may use at most 192 MiB of HBM per device.

v0:
```python
import math

import jax
import jax.numpy as jnp
from jax import lax
from jax.sharding import PartitionSpec as P

D = 768
HEADS = 12
HD = 64
FF = 2304
C = 768
SIDE = 16
STEP = 10
SEQ = 256


NORM_EPS = 1e-06
COS_EPS = 1e-06
SIGMA_DATA = 0.5
BETA_ONE = 0.5
BETA_TWO = 0.5
ADAM_EPS = 1e-08
WEIGHT_DECAY = 0.01
LEARN_RATE = 0.04
SCALE_RATE = 1.0
ROOT_HALF = 0.7071067811865476
INV_ROOT_TWO_PI = 0.3989422804014327


def dot_rows(left, right):
    return lax.dot_general(
        left, right, (((1,), (1,)), ((), ())), preferred_element_type=jnp.float32
    )


def dot_cols(left, right):
    return lax.dot_general(
        left, right, (((0,), (0,)), ((), ())), preferred_element_type=jnp.float32
    )


def slot_places(owner_list, slots):
    unit_count = owner_list.shape[0]
    same_owner = owner_list[:, None] == owner_list[None, :]
    row_ids = lax.broadcasted_iota(jnp.int32, (unit_count, unit_count), 0)
    col_ids = lax.broadcasted_iota(jnp.int32, (unit_count, unit_count), 1)
    before = jnp.sum(jnp.where(same_owner & (col_ids < row_ids), 1, 0), axis=1).astype(jnp.int32)
    return owner_list * slots + before


def rope_tables(positions, first_head, heads_here):
    quarter = HD // 8
    head_ids = lax.broadcasted_iota(jnp.int32, (heads_here, quarter), 0) + first_head
    column = lax.broadcasted_iota(jnp.int32, (heads_here, quarter), 1)
    flat_index = (column * HEADS + head_ids).astype(jnp.float32)
    low_log = math.log(math.pi)
    high_log = math.log(10.0 * math.pi)
    frequency = jnp.exp(low_log + (high_log - low_log) * flat_index / (HEADS * quarter))
    placed = (2.0 * positions.astype(jnp.float32) + 1.0) / SIDE - 1.0
    along_rows = placed[:, 0, :, None, None] * frequency[None, None]
    along_cols = placed[:, 1, :, None, None] * frequency[None, None]
    angles = jnp.concatenate([along_rows, along_cols], axis=-1)
    return (jnp.cos(angles), jnp.sin(angles))


def rotate(field, cosine, sine_table):
    span_width = cosine.shape[-1]
    first_part = field[..., :span_width]
    second = field[..., span_width : 2 * span_width]
    return jnp.concatenate(
        [
            first_part * cosine - second * sine_table,
            second * cosine + first_part * sine_table,
            field[..., 2 * span_width :],
        ],
        axis=-1,
    )


def unrotate(field, cosine, sine_table):
    span_width = cosine.shape[-1]
    first_part = field[..., :span_width]
    second = field[..., span_width : 2 * span_width]
    return jnp.concatenate(
        [
            first_part * cosine + second * sine_table,
            second * cosine - first_part * sine_table,
            field[..., 2 * span_width :],
        ],
        axis=-1,
    )


def attention_side(normed, in_proj, scale_root, cosine, sine_table, images):
    projected = dot_rows(normed, in_proj)
    feat_rows = in_proj.shape[0] // 3
    head_shape = (images, SEQ, feat_rows // HD, HD)
    query_raw = projected[:, :feat_rows].reshape(head_shape)
    key_raw = projected[:, feat_rows : 2 * feat_rows].reshape(head_shape)
    value_low = projected[:, 2 * feat_rows :].reshape(head_shape).astype(jnp.bfloat16)
    query_inverse = lax.rsqrt(jnp.sum(query_raw * query_raw, axis=-1, keepdims=True) + COS_EPS)
    key_inverse = lax.rsqrt(jnp.sum(key_raw * key_raw, axis=-1, keepdims=True) + COS_EPS)
    query_low = rotate(query_raw * scale_root * query_inverse, cosine, sine_table).astype(
        jnp.bfloat16
    )
    key_low = rotate(key_raw * scale_root * key_inverse, cosine, sine_table).astype(jnp.bfloat16)
    return (query_raw, key_raw, query_inverse, key_inverse, query_low, key_low, value_low)


def attend(query_low, key_low, value_low):
    scores = jnp.einsum("ishd,ithd->ihst", query_low, key_low, preferred_element_type=jnp.float32)
    top_score = jnp.max(scores, axis=-1, keepdims=True)
    exp_scores = jnp.exp(scores - top_score)
    row_total = jnp.sum(exp_scores, axis=-1, keepdims=True)
    probs_low = (exp_scores / row_total).astype(jnp.bfloat16)
    mixed_out = jnp.einsum(
        "ihst,ithd->ishd", probs_low, value_low, preferred_element_type=jnp.float32
    )
    return (mixed_out, top_score + jnp.log(row_total))


def norm_back(grad_normed, x_block, inverse, gain_rows):
    scaled = grad_normed * gain_rows[:, None, :]
    grad_x = inverse * scaled - x_block * inverse * inverse * inverse * jnp.mean(
        x_block * scaled, axis=-1, keepdims=True
    )
    grad_gain = jnp.sum(grad_normed * x_block * inverse, axis=1)
    return (grad_x, grad_gain)


def adam_step(weights, first_new, second_new, rate):
    fix_one = 1.0 - math.pow(BETA_ONE, STEP)
    fix_two = 1.0 - math.pow(BETA_TWO, STEP)
    return weights * (1.0 - rate * WEIGHT_DECAY) - rate * (first_new / fix_one) / (
        jnp.sqrt(second_new / fix_two) + ADAM_EPS
    )


def on_device(
    tokens,
    conditioning,
    sigmas,
    positions,
    cotangent,
    owners,
    master,
    moment_one,
    moment_two,
    scale_state,
):
    dp_count = lax.axis_size("dp")
    mp_count = lax.axis_size("mp")
    mp_index = lax.axis_index("mp")
    images = conditioning.shape[0]
    tok_rows = tokens.shape[0]
    slots = master.shape[1]
    unit_rows = master.shape[2]
    unit_count = owners.shape[1]
    heads_here = scale_state.shape[1]
    cond_rows = C // mp_count
    feat_rows = D // mp_count
    hidden_rows = FF // mp_count
    placed = slot_places(owners[0], slots)

    def unpack(gathered):
        rows_all = gathered.reshape(unit_count * unit_rows, D)
        row_counts = [cond_rows, 3 * feat_rows, feat_rows, cond_rows, 2 * hidden_rows, hidden_rows]
        pieces = []
        row_start = 0
        for span_rows in row_counts:
            pieces.append(rows_all[row_start : row_start + span_rows])
            row_start += span_rows
        return pieces

    rounded = master[0].astype(jnp.bfloat16).reshape(slots, unit_rows * D)
    dealt = lax.all_to_all(rounded, "dp", split_axis=1, concat_axis=0, tiled=True)
    shards = jnp.take(dealt, placed, axis=0)
    ada_first, in_proj, out_proj, ada_second, gate_up, down_proj = unpack(
        lax.all_gather(shards, "dp", axis=1, tiled=True)
    )
    cond_low = conditioning.astype(jnp.bfloat16)
    cond_half = lax.dynamic_slice_in_dim(cond_low, mp_index * cond_rows, cond_rows, 1)
    gain_first, gain_second = lax.psum(
        (
            jnp.dot(cond_half, ada_first, preferred_element_type=jnp.float32),
            jnp.dot(cond_half, ada_second, preferred_element_type=jnp.float32),
        ),
        "mp",
    )
    gain_first = 1.0 + gain_first
    gain_second = 1.0 + gain_second
    x_full = tokens.reshape(images, SEQ, D)
    norm_first = lax.rsqrt(jnp.mean(x_full * x_full, axis=-1, keepdims=True) + NORM_EPS)
    normed_first = (
        (x_full * norm_first * gain_first[:, None, :]).astype(jnp.bfloat16).reshape(tok_rows, D)
    )
    scale_root = jnp.sqrt(scale_state[0])[None, None, :, None]
    cosine, sine_table = rope_tables(positions, mp_index * heads_here, heads_here)
    attention_parts = attention_side(normed_first, in_proj, scale_root, cosine, sine_table, images)
    mixed_out, log_total = attend(attention_parts[4], attention_parts[5], attention_parts[6])
    mixed_low = mixed_out.reshape(tok_rows, feat_rows).astype(jnp.bfloat16)
    attn_out = lax.psum(jnp.dot(mixed_low, out_proj, preferred_element_type=jnp.float32), "mp")
    x_mid = tokens + attn_out
    mid_block = x_mid.reshape(images, SEQ, D)
    norm_second = lax.rsqrt(jnp.mean(mid_block * mid_block, axis=-1, keepdims=True) + NORM_EPS)
    normed_second = (
        (mid_block * norm_second * gain_second[:, None, :])
        .astype(jnp.bfloat16)
        .reshape(tok_rows, D)
    )
    gate_vals = dot_rows(normed_second, gate_up)
    gate_part = gate_vals[:, :hidden_rows]
    up_part = gate_vals[:, hidden_rows:]
    hidden_low = (jax.nn.gelu(gate_part, approximate=False) * up_part).astype(jnp.bfloat16)
    ff_out = lax.psum(
        jnp.dot(hidden_low, down_proj, preferred_element_type=jnp.float32).astype(jnp.bfloat16),
        "mp",
    ).astype(jnp.float32)
    output = x_mid + ff_out
    square = sigmas * sigmas
    data_square = SIGMA_DATA * SIGMA_DATA
    loss_weight = 4.0 * square * data_square / ((square + data_square) * (square + data_square))
    grad_out = (
        cotangent.astype(jnp.float32).reshape(images, SEQ, D) * loss_weight[:, None, None]
    ).reshape(tok_rows, D)
    regathered = unpack(lax.all_gather(shards, "dp", axis=1, tiled=True))
    back_in, back_out, back_gu, back_down = (
        regathered[1],
        regathered[2],
        regathered[4],
        regathered[5],
    )
    normed_back = (
        (x_full * norm_first * gain_first[:, None, :]).astype(jnp.bfloat16).reshape(tok_rows, D)
    )
    attn_back = attention_side(normed_back, back_in, scale_root, cosine, sine_table, images)
    second_back = (
        (mid_block * norm_second * gain_second[:, None, :])
        .astype(jnp.bfloat16)
        .reshape(tok_rows, D)
    )
    gate_again = dot_rows(second_back, back_gu)
    gate_back = gate_again[:, :hidden_rows]
    up_back = gate_again[:, hidden_rows:]
    hidden_back = (jax.nn.gelu(gate_back, approximate=False) * up_back).astype(jnp.bfloat16)
    grad_low = grad_out.astype(jnp.bfloat16)
    grad_hidden = dot_rows(grad_low, back_down)
    grad_down = dot_cols(hidden_back, grad_low)
    gelu_gate = jax.nn.gelu(gate_back, approximate=False)
    gelu_slope = 0.5 * (
        1.0 + lax.erf(gate_back * ROOT_HALF)
    ) + gate_back * INV_ROOT_TWO_PI * jnp.exp(-0.5 * gate_back * gate_back)
    grad_gu = jnp.concatenate(
        [grad_hidden * up_back * gelu_slope, grad_hidden * gelu_gate], axis=1
    ).astype(jnp.bfloat16)
    grad_gate_up = dot_cols(grad_gu, second_back)
    grad_normed_second = lax.psum(
        jnp.dot(grad_gu, back_gu, preferred_element_type=jnp.float32), "mp"
    )
    grad_mid_norm, grad_gain_second = norm_back(
        grad_normed_second.reshape(images, SEQ, D), mid_block, norm_second, gain_second
    )
    grad_mid = grad_out + grad_mid_norm.reshape(tok_rows, D)
    query_raw, key_raw, query_inverse, key_inverse, query_low, key_low, value_low = attn_back
    scores = jnp.einsum("ishd,ithd->ihst", query_low, key_low, preferred_element_type=jnp.float32)
    probs = jnp.exp(scores - log_total)
    probs_low = probs.astype(jnp.bfloat16)
    mixed_back = (
        jnp.einsum("ihst,ithd->ishd", probs_low, value_low, preferred_element_type=jnp.float32)
        .reshape(tok_rows, feat_rows)
        .astype(jnp.bfloat16)
    )
    branch_low = grad_mid.astype(jnp.bfloat16)
    grad_out_proj = dot_cols(mixed_back, branch_low)
    grad_mixed = dot_rows(branch_low, back_out).astype(jnp.bfloat16).reshape(query_low.shape)
    grad_probs = jnp.einsum(
        "ishd,ithd->ihst", grad_mixed, value_low, preferred_element_type=jnp.float32
    )
    inner_sum = jnp.sum(probs * grad_probs, axis=-1, keepdims=True)
    grad_scores = (probs * (grad_probs - inner_sum)).astype(jnp.bfloat16)
    grad_query_hat = jnp.einsum(
        "ihst,ithd->ishd", grad_scores, key_low, preferred_element_type=jnp.float32
    )
    grad_key_hat = jnp.einsum(
        "ihst,ishd->ithd", grad_scores, query_low, preferred_element_type=jnp.float32
    )
    grad_value = jnp.einsum(
        "ihst,ishd->ithd", probs_low, grad_mixed, preferred_element_type=jnp.float32
    )
    grad_query_n = unrotate(grad_query_hat, cosine, sine_table)
    grad_key_n = unrotate(grad_key_hat, cosine, sine_table)
    query_unit = query_raw * query_inverse
    key_unit = key_raw * key_inverse
    grad_query = (
        scale_root
        * query_inverse
        * (grad_query_n - query_unit * jnp.sum(query_unit * grad_query_n, axis=-1, keepdims=True))
    )
    grad_key = (
        scale_root
        * key_inverse
        * (grad_key_n - key_unit * jnp.sum(key_unit * grad_key_n, axis=-1, keepdims=True))
    )
    scale_part = jnp.sum(grad_query_n * query_unit + grad_key_n * key_unit, axis=(0, 1, 3)) / (
        2.0 * jnp.sqrt(scale_state[0])
    )
    grad_proj = jnp.concatenate(
        [
            grad_query.reshape(tok_rows, feat_rows),
            grad_key.reshape(tok_rows, feat_rows),
            grad_value.reshape(tok_rows, feat_rows),
        ],
        axis=1,
    ).astype(jnp.bfloat16)
    grad_in_proj = dot_cols(grad_proj, normed_back)
    grad_normed_first = lax.psum(
        jnp.dot(grad_proj, back_in, preferred_element_type=jnp.float32), "mp"
    )
    grad_x_norm, grad_gain_first = norm_back(
        grad_normed_first.reshape(images, SEQ, D), x_full, norm_first, gain_first
    )
    input_grad = grad_mid + grad_x_norm.reshape(tok_rows, D)
    cond_wide = cond_half.astype(jnp.float32)
    grad_ada_first = lax.dot_general(
        cond_wide,
        grad_gain_first,
        (((0,), (0,)), ((), ())),
        precision=lax.Precision.HIGHEST,
        preferred_element_type=jnp.float32,
    )
    grad_ada_second = lax.dot_general(
        cond_wide,
        grad_gain_second,
        (((0,), (0,)), ((), ())),
        precision=lax.Precision.HIGHEST,
        preferred_element_type=jnp.float32,
    )
    local_grads = jnp.concatenate(
        [grad_ada_first, grad_in_proj, grad_out_proj, grad_ada_second, grad_gate_up, grad_down],
        axis=0,
    ).reshape(unit_count, unit_rows * D)
    scale_rows = jnp.broadcast_to(scale_part[None, None, :], (1, dp_count, heads_here))
    grad_shards, scale_grad = (
        lax.psum_scatter(local_grads, "dp", scatter_dimension=1, tiled=True),
        lax.psum_scatter(scale_rows, "dp", scatter_dimension=1, tiled=True),
    )
    total_slots = dp_count * slots
    slot_ids = lax.broadcasted_iota(jnp.int32, (total_slots, unit_count), 0)
    unit_ids = lax.broadcasted_iota(jnp.int32, (total_slots, unit_count), 1)
    match_table = slot_ids == placed[None, :]
    source_unit = jnp.sum(jnp.where(match_table, unit_ids, 0), axis=1)
    filled = jnp.any(match_table, axis=1)
    outgoing = jnp.where(filled[:, None], jnp.take(grad_shards, source_unit, axis=0), 0.0)
    owned_grads = lax.all_to_all(outgoing, "dp", split_axis=0, concat_axis=1, tiled=True).reshape(
        slots, unit_rows, D
    )
    first_new = BETA_ONE * moment_one[0] + (1.0 - BETA_ONE) * owned_grads
    second_new = BETA_TWO * moment_two[0] + (1.0 - BETA_TWO) * owned_grads * owned_grads
    master_new = adam_step(master[0], first_new, second_new, LEARN_RATE)
    scale_grad = scale_grad.reshape(heads_here)
    scale_first = BETA_ONE * scale_state[1] + (1.0 - BETA_ONE) * scale_grad
    scale_second = BETA_TWO * scale_state[2] + (1.0 - BETA_TWO) * scale_grad * scale_grad
    scale_new = adam_step(scale_state[0], scale_first, scale_second, SCALE_RATE)
    scale_update = jnp.stack([scale_first, scale_new])
    return (
        output,
        input_grad,
        grad_shards[None],
        master_new[None],
        first_new[None],
        second_new[None],
        scale_update,
        scale_second,
    )


def solution(mesh):
    in_specs = (
        P("dp", None),
        P("dp", None),
        P("dp"),
        P("dp", None, None),
        P("dp", None),
        P("mp", None),
        P("mp", "dp", None, None),
        P("mp", "dp", None, None),
        P("mp", "dp", None, None),
        P(None, "mp"),
    )
    out_specs = (
        P("dp", None),
        P("dp", None),
        P("mp", None, "dp"),
        P("mp", "dp", None, None),
        P("mp", "dp", None, None),
        P("mp", "dp", None, None),
        P(None, "mp"),
        P("mp"),
    )
    return jax.shard_map(
        on_device, mesh=mesh, in_specs=in_specs, out_specs=out_specs, check_vma=False
    )
```

profile of v0, /device:TPU:0, one launch (start us, length us, event | category | flops | bytes accessed | tf_op | source)
XLA Modules:
  0.0 915.7 jit_solution(1860011402872100253)
XLA Ops:
  10.0 7.4 all-to-all-start
  17.6 18.4 %all-to-all-done = bf16[12,16,1536]{2,0,1:T(8,128)(2,1)S(1)} async-done(((bf16[12,16,1536]{2,0,1:T(8,128)(2,1)}), bf16[12,16,1536]{2,0,1:T(8,128)(2,1)S(1)}, u32[]{:S(2)}, u32[]{:S(2)}) %all-to-all-start) | async-done | bytes 589856 | tf_op jit(solution)/shard_map/all_to_all | solution.py:177
  44.5 78.2 %all-gather.2.cloned.1.call-done = bf16[180,24576]{1,0:T(8,128)(2,1)} async-done(((bf16[180,1536]{1,0:T(8,128)(2,1)}), bf16[180,24576]{1,0:T(8,128)(2,1)}) %all-gather.2.cloned.1.call-update) | async-done | bytes 8847376 | tf_op jit(solution)/shard_map/all_gather | solution.py:180
  134.6 9.6 %all-reduce.1 = (f32[4,768]{1,0:T(4,128)}, f32[4,768]{1,0:T(4,128)}) all-reduce(f32[4,768]{1,0:T(4,128)} %fusion.64, f32[4,768]{1,0:T(4,128)} %fusion.63), channel_id=1, replica_groups=mesh['dp'=16,'mp'=2] {'mp'}, use_global_device_ids=true, to_apply=%region_2.3 | all-reduce | flops 6144 | bytes 49152 | tf_op jit(solution)/shard_map/psum | solution.py:184
  145.6 4.6 fusion.56
  196.6 4.1 slice.175
  200.6 5.8 slice.143
  210.9 68.1 %all-reduce.7.cloned.1.call-done = f32[1024,768]{1,0:T(8,128)} async-done(((f32[1024,768]{1,0:T(8,128)}), f32[1024,768]{1,0:T(8,128)}) %all-reduce.7.cloned.1.call-update) | async-done | bytes 3145744 | tf_op jit(solution)/shard_map/psum | solution.py:203
  288.6 14.9 %multiply_convert_fusion.1 = (bf16[1024,1152]{1,0:T(8,128)(2,1)}, f32[1024,1152]{1,0:T(8,128)S(1)}, bf16[1024,1152]{1,0:T(8,128)(2,1)}) fusion(f32[1024,2304]{1,0:T(8,128)S(1)} %fusion.67, bf16[1152,768]{1,0:T(8,128)(2,1)S(1)} %copy-done.36, bf16[1024,768]{1,0:T(8,128)(2,1)S(1)} %copy-done.49, f32[1024]{0:T(1024)S(1)} %bitcast.185), kind=kOutput, calls=%fused_computation.24 | convolution fusion | flops 1905131520 | bytes 22220800 | tf_op jit(solution)/shard_map/dot_general | solution.py:32
  309.4 7.9 fusion.20
  329.5 31.1 %all-reduce.9.cloned.1.call-done = bf16[1024,768]{1,0:T(8,128)(2,1)} async-done(((bf16[1024,768]{1,0:T(8,128)(2,1)}), bf16[1024,768]{1,0:T(8,128)(2,1)}) %all-reduce.9.cloned.1.call-update) | async-done | bytes 1572880 | tf_op jit(solution)/shard_map/psum | solution.py:216
  360.6 88.5 %all-reduce.11.cloned.1.call-done = f32[1024,768]{1,0:T(8,128)} async-done(((f32[1024,768]{1,0:T(8,128)}), f32[1024,768]{1,0:T(8,128)}) %all-reduce.11.cloned.1.call-update) | async-done | bytes 3145744 | tf_op jit(solution)/shard_map/psum | solution.py:258
  449.1 5.9 fusion.58
  462.5 4.9 fusion.23
  498.1 5.7 add_reduce_fusion
  517.9 76.9 %all-reduce.13.cloned.1.call-done = f32[1024,768]{1,0:T(8,128)} async-done(((f32[1024,768]{1,0:T(8,128)}), f32[1024,768]{1,0:T(8,128)}) %all-reduce.13.cloned.1.call-update) | async-done | bytes 3145744 | tf_op jit(solution)/shard_map/psum | solution.py:317
  607.2 6.8 convolution_dynamic-update-slice_fusion
  614.0 3.9 convolution_dynamic-update-slice_fusion.1
  617.9 17.5 %reshape.376 = f32[180,24576]{1,0:T(8,128)} reshape(f32[5760,768]{1,0:T(8,128)} %convolution_dynamic-update-slice_fusion.1) | data formatting | bytes 35389440 | tf_op jit(solution)/shard_map/reshape | solution.py:342
  636.6 187.5 %reduce-scatter.3.cloned.1.call-done = f32[180,1536]{1,0:T(8,128)} async-done(((f32[180,24576]{1,0:T(8,128)}), f32[180,1536]{1,0:T(8,128)}) %reduce-scatter.3.cloned.1.call-update) | async-done | bytes 1105936 | tf_op jit(solution)/shard_map/reduce_scatter | solution.py:345
  833.3 4.4 all-to-all-start.1
  838.5 53.3 %all-reduce = f32[1,16,6]{2,1,0:T(8,128)S(1)} all-reduce(f32[1,16,6]{2,1,0:T(8,128)S(1)} %broadcast_in_dim.94), channel_id=3, replica_groups=mesh['dp'=16,'mp'=2] {'dp'}, use_global_device_ids=true, to_apply=%region_25.26.clone | all-reduce | flops 96 | bytes 768
  894.3 5.6 subtract_add_fusion
  904.3 4.1 divide_subtract_fusion
  (360 shorter events, 184.7 us)
Async XLA Ops:
  7.2 123.7 %copy-start = (f32[4,768]{1,0:T(4,128)S(1)}, f32[4,768]{1,0:T(4,128)}, u32[]{:S(2)}) copy-start(f32[4,768]{1,0:T(4,128)} %param.11) | copy-start | bytes 36868
  7.2 10.2 %copy-start.84 = (s32[1,180]{1,0:T(1,128)S(1)}, s32[1,180]{1,0:T(1,128)}, u32[]{:S(2)}) copy-start(s32[1,180]{1,0:T(1,128)} %param.15) | copy-start | bytes 2164
  10.0 26.1 %all-to-all-start = ((bf16[12,16,1536]{2,0,1:T(8,128)(2,1)}), bf16[12,16,1536]{2,0,1:T(8,128)(2,1)S(1)}, u32[]{:S(2)}, u32[]{:S(2)}) async-start(bf16[12,16,1536]{2,0,1:T(8,128)(2,1)} %copy.166), calls=%async_computation | async-start | bytes 1572864 | tf_op jit(solution)/shard_map/all_to_all | solution.py:177
  17.3 105.4 %all-gather.2.cloned.1.call-start = ((), (), s32[]{:S(2)}) async-start(), calls=%async_computation.3 | async-start | bytes 9609216 | tf_op jit(solution)/shard_map/all_gather | solution.py:180
  17.6 18.5 %copy-start.89 = (s32[180]{0:T(256)}, s32[180]{0:T(256)S(1)}, u32[]{:S(2)}) copy-start(s32[180]{0:T(256)S(1)} %select_reduce_fusion.1) | copy-start | bytes 2164
  37.0 7.0 copy-start.3
  42.7 236.4 %all-reduce.7.cloned.1.call-start = ((), (), s32[]{:S(2)}) async-start(), calls=%async_computation.4 | async-start | bytes 6291456 | tf_op jit(solution)/shard_map/psum | solution.py:203
  44.3 109.6 %copy-start.82 = (f32[1024]{0:T(1024)}, f32[1024]{0:T(1024)S(1)}, u32[]{:S(2)}) copy-start(f32[1024]{0:T(1024)S(1)} %add_rsqrt_fusion.3) | copy-start | bytes 12292
  44.5 140.7 %copy-start.41 = (f32[4,256,6,8]{1,3,2,0:T(8,128)}, f32[4,256,6,8]{1,3,2,0:T(8,128)S(1)}, u32[]{:S(2)}) copy-start(f32[4,256,6,8]{1,3,2,0:T(8,128)S(1)} %get-tuple-element.97) | copy-start | bytes 589828
  44.5 140.7 %copy-start.43 = (f32[4,256,6,8]{1,3,2,0:T(8,128)}, f32[4,256,6,8]{1,3,2,0:T(8,128)S(1)}, u32[]{:S(2)}) copy-start(f32[4,256,6,8]{1,3,2,0:T(8,128)S(1)} %get-tuple-element.98) | copy-start | bytes 589828
  195.8 164.7 %all-reduce.9.cloned.1.call-start = ((), (), s32[]{:S(2)}) async-start(), calls=%async_computation.5 | async-start | bytes 3145728 | tf_op jit(solution)/shard_map/psum | solution.py:216
  308.9 140.2 %all-reduce.11.cloned.1.call-start = ((), (), s32[]{:S(2)}) async-start(), calls=%async_computation.6 | async-start | bytes 6291456 | tf_op jit(solution)/shard_map/psum | solution.py:258
  317.3 277.5 %all-reduce.13.cloned.1.call-start = ((), (), s32[]{:S(2)}) async-start(), calls=%async_computation.7 | async-start | bytes 6291456 | tf_op jit(solution)/shard_map/psum | solution.py:317
  324.8 124.3 %copy-start.8 = (f32[1024,768]{1,0:T(8,128)S(1)}, f32[1024,768]{1,0:T(8,128)}, u32[]{:S(2)}) copy-start(f32[1024,768]{1,0:T(8,128)} %copy-done.7) | copy-start | bytes 9437188
  324.8 124.3 %copy-start.76 = (f32[4,768]{1,0:T(4,128)S(1)}, f32[4,768]{1,0:T(4,128)}, u32[]{:S(2)}) copy-start(f32[4,768]{1,0:T(4,128)} %broadcast_add_fusion) | copy-start | bytes 36868
  329.5 139.7 %copy-start.57 = (f32[4,6,256]{2,1,0:T(8,128)}, f32[4,6,256]{2,1,0:T(8,128)S(1)}, u32[]{:S(2)}) copy-start(f32[4,6,256]{2,1,0:T(8,128)S(1)} %log_add_fusion) | copy-start | bytes 73732
  329.5 125.6 %copy-start.87 = (f32[1,2,4,128]{3,1,2,0:T(2,128)S(1)}, f32[1,2,4,128]{3,1,2,0:T(2,128)}, u32[]{:S(2)}) copy-start(f32[1,2,4,128]{3,1,2,0:T(2,128)} %copy.221) | copy-start | bytes 12292
  458.4 9.0 slice-start
  508.8 315.3 %reduce-scatter.3.cloned.1.call-start = ((), (), s32[]{:S(2)}) async-start(), calls=%async_computation.8 | async-start | bytes 19218432 | tf_op jit(solution)/shard_map/reduce_scatter | solution.py:345
  513.8 81.0 %copy-start.4 = (f32[1024,768]{1,0:T(8,128)S(1)}, f32[1024,768]{1,0:T(8,128)}, u32[]{:S(2)}) copy-start(f32[1024,768]{1,0:T(8,128)} %param.10) | copy-start | bytes 9437188
  513.8 81.0 %copy-start.74 = (f32[4,768]{1,0:T(4,128)S(1)}, f32[4,768]{1,0:T(4,128)}, u32[]{:S(2)}) copy-start(f32[4,768]{1,0:T(4,128)} %broadcast_add_fusion.1) | copy-start | bytes 36868
  830.4 7.3 copy-start.96
  830.4 8.0 copy-start.94
  833.3 68.7 %all-to-all-start.1 = ((f32[16,12,1536]{2,1,0:T(8,128)}), f32[16,12,1536]{2,1,0:T(8,128)}, u32[]{:S(2)}, u32[]{:S(2)}) async-start(f32[16,12,1536]{2,1,0:T(8,128)} %select_select_fusion), calls=%async_computation.2 | async-start | bytes 3145728 | tf_op jit(solution)/shard_map/all_to_all | solution.py:355
  (86 other events, 255.1 us)
Sparse Core Ops, SparseCore 0:
  42.8 79.8 all-gather.1
  196.0 83.0 all-reduce.6
  309.1 51.4 all-reduce.8
  363.3 85.7 all-reduce.10
  509.0 85.7 all-reduce.12
  635.6 188.4 reduce-scatter.2
where the time goes:
time: 922 us; the launch traced here: 916 us
  waiting for transfers between devices  549 us (60%)
  local copies, waits for them, and re-layouts  138 us (15%)
  matrix products  77.8 us (8%)
  blocking collectives  63 us (7%)
  other arithmetic  59.1 us (6%)
  between operations  15.9 us (2%)
  starting transfers between devices  12.7 us (1%)
    reduce_scatter x1, waiting for transfers between devices, on_device(): lax.psum_scatter(local_grads, 'dp', scatter_dimension=1, tiled=True)  188 us
    psum x1, waiting for transfers between devices, on_device(): lax.psum(jnp.dot(grad_gu, back_gu, preferred_element_type=jnp.float32), '...  88.5 us
    all_gather x1, waiting for transfers between devices, on_device(): lax.all_gather(shards, 'dp', axis=1, tiled=True)  78.2 us
    psum x1, waiting for transfers between devices, on_device(): lax.psum(jnp.dot(grad_proj, back_in, preferred_element_type=jnp.float32),...  76.9 us
    psum x1, waiting for transfers between devices, on_device(): lax.psum(jnp.dot(mixed_low, out_proj, preferred_element_type=jnp.float32)...  68.1 us
    unnamed x1, blocking collectives  53.3 us
    slice x9, local copies, waits for them, and re-layouts, unpack(): pieces.append(rows_all[row_start:row_start + span_rows])  32.7 us
    psum x1, waiting for transfers between devices, on_device(): lax.psum(jnp.dot(hidden_low, down_proj, preferred_element_type=jnp.float3...  31.1 us
  transfers between devices with their start and end apart: 8, of which 7 were waited for; matrix products, arithmetic and copies ran while one was open for 6% of the time, Pallas kernels for 0%

commit v1 on v0

v1 whole, which is shorter than its diff:
```python
import math

import jax
import jax.numpy as jnp
from jax import lax
from jax.experimental import pallas as pl
from jax.experimental.pallas import tpu as pltpu
from jax.sharding import PartitionSpec as P

D = 768
HEADS = 12
HD = 64
FF = 2304
SIDE = 16
STEP = 10
SEQ = 256
UNIT = 32
SPAN = 12
CHUNK = SPAN * UNIT
HALF_CHUNK = CHUNK // 2

NORM_EPS = 1e-06
COS_EPS = 1e-06
SIGMA_DATA = 0.5
BETA_ONE = 0.5
BETA_TWO = 0.5
ADAM_EPS = 1e-08
WEIGHT_DECAY = 0.01
LEARN_RATE = 0.04
SCALE_RATE = 1.0
ROOT_HALF = 0.7071067811865476
INV_ROOT_TWO_PI = 0.3989422804014327

F32 = jnp.float32
BF16 = jnp.bfloat16
VMEM_BYTES = 60 * 1024 * 1024

STACK_ORDER = ("A1", "Q", "K", "V", "O", "A2", "G", "G", "G", "U", "U", "U", "F", "F", "F")
ROW_A1, ROW_A2, ROW_Q, ROW_K, ROW_V, ROW_O = (D * place for place in range(6))
ROW_G = 6 * D
ROW_U = ROW_G + FF
ROW_F = ROW_U + FF
ROWS_ALL = ROW_F + FF


def dot_nn(left, right):
    return jnp.dot(left, right, preferred_element_type=F32)


def dot_nt(left, right):
    return lax.dot_general(left, right, (((1,), (1,)), ((), ())), preferred_element_type=F32)


def slots_before(owner_list):
    unit_count = owner_list.shape[0]
    same_owner = owner_list[:, None] == owner_list[None, :]
    row_ids = lax.broadcasted_iota(jnp.int32, (unit_count, unit_count), 0)
    col_ids = lax.broadcasted_iota(jnp.int32, (unit_count, unit_count), 1)
    return jnp.sum(jnp.where(same_owner & (col_ids < row_ids), 1, 0), axis=1).astype(jnp.int32)


def rope_tables(positions):
    quarter = HD // 8
    head_ids = lax.broadcasted_iota(jnp.int32, (HEADS, quarter), 0)
    column = lax.broadcasted_iota(jnp.int32, (HEADS, quarter), 1)
    flat_index = (column * HEADS + head_ids).astype(F32)
    low_log = math.log(math.pi)
    high_log = math.log(10.0 * math.pi)
    frequency = jnp.exp(low_log + (high_log - low_log) * flat_index / (HEADS * quarter))
    placed = (2.0 * positions.astype(F32) + 1.0) / SIDE - 1.0
    along_rows = placed[:, 0].reshape(1, 1, -1) * frequency[:, :, None]
    along_cols = placed[:, 1].reshape(1, 1, -1) * frequency[:, :, None]
    angles = jnp.concatenate([along_rows, along_cols], axis=1).reshape(HEADS * 2 * quarter, -1)
    return jnp.cos(angles), jnp.sin(angles)


def deal_matrix(core):
    target = lax.broadcasted_iota(jnp.int32, (CHUNK, CHUNK), 0)
    source = lax.broadcasted_iota(jnp.int32, (CHUNK, CHUNK), 1)
    parity = (target // HALF_CHUNK + core) % 2
    inner = target % HALF_CHUNK
    piece = inner // (2 * SPAN)
    row = inner // SPAN % 2
    unit = inner % SPAN
    return (source == unit * UNIT + 4 * piece + 2 * parity + row).astype(BF16)


def layer_kernel(
    images,
    src_ref,
    scal_ref,
    x_ref,
    cot_ref,
    cond_ref,
    cos_ref,
    sin_ref,
    deal_ref,
    slots_ref,
    out_hbm,
    grad_hbm,
    hid_keep,
    hid_send,
    gu_keep,
    gu_send,
    at_keep,
    at_send,
    n1_hbm,
    n2_hbm,
    gb_hbm,
    ga_hbm,
    gain_hbm,
    ds_hbm,
    w,
    unit_s,
    coef_s,
    qtok_s,
    qk_s,
    v_s,
    o_s,
    x2_s,
    n1_s,
    n2_s,
    gb_s,
    ga_s,
    do_s,
    dot_s,
    ff_s,
    dn2_s,
    dqkv_s,
    hid_s,
    gu_s,
    at_s,
    out_s,
    gin_s,
    gain_s,
    ds_s,
    dsout_s,
    w_sem,
    o_sem,
):
    toks = images * SEQ
    sends = []

    def send(src, dst):
        copy = pltpu.make_async_copy(src, dst, o_sem.at[len(sends)])
        copy.start()
        sends.append(copy)

    groups = ((0, ROW_Q), (ROW_Q, ROW_O), (ROW_O, ROW_G), (ROW_G, ROWS_ALL))
    for index, (low, high) in enumerate(groups):

        @pl.loop(low // UNIT, high // UNIT)
        def _(unit):
            pltpu.make_async_copy(
                slots_ref.at[src_ref[unit]],
                w.at[pl.ds(pl.multiple_of(unit * UNIT, UNIT), UNIT)],
                w_sem.at[index],
            ).start()

    def weights_here(index):
        low, high = groups[index]
        region = w.at[pl.ds(low, high - low)]
        pltpu.make_async_copy(region, region, w_sem.at[index]).wait()

    def image_rows(image):
        return pl.ds(image * SEQ, SEQ)

    weights_here(0)
    gain_one = 1.0 + dot_nn(cond_ref[...], w[ROW_A1 : ROW_A1 + D])
    gain_two = 1.0 + dot_nn(cond_ref[...], w[ROW_A2 : ROW_A2 + D])
    for image in range(images):
        x = x_ref[image_rows(image)]
        inverse = lax.rsqrt(jnp.mean(x * x, axis=-1, keepdims=True) + NORM_EPS)
        n1_s[image_rows(image)] = (x * inverse * gain_one[image : image + 1]).astype(BF16)
        weight = scal_ref[2 * HEADS + image]
        gb_s[image_rows(image)] = (cot_ref[image_rows(image)].astype(F32) * weight).astype(BF16)
    send(n1_s, n1_hbm)
    send(gb_s, gb_hbm)
    weights_here(1)
    unit_s[:D] = dot_nt(w[ROW_Q : ROW_Q + D], n1_s[...])
    unit_s[D:] = dot_nt(w[ROW_K : ROW_K + D], n1_s[...])
    v_s[...] = dot_nt(w[ROW_V : ROW_V + D], n1_s[...]).astype(BF16)

    @pl.loop(0, 2 * HEADS)
    def _(index):
        head = lax.rem(index, HEADS)
        rows = pl.ds(pl.multiple_of(index * HD, HD), HD)
        angle_rows = pl.ds(pl.multiple_of(head * 16, 16), 16)
        raw = unit_s[rows]
        inverse = lax.rsqrt(jnp.sum(raw * raw, axis=0, keepdims=True) + COS_EPS)
        unit = raw * inverse
        root = scal_ref[HEADS + head]
        unit_s[rows] = unit
        coef_s[pl.ds(index, 1)] = root * inverse
        scaled = unit * root
        first, second = scaled[:16], scaled[16:32]
        cosine, sine = cos_ref[angle_rows], sin_ref[angle_rows]
        turned = jnp.concatenate(
            [first * cosine - second * sine, second * cosine + first * sine, scaled[32:]], axis=0
        )
        qk_s[rows] = turned.astype(BF16)

    qtok_s[...] = qk_s[:D].T

    def pair_parts(image, pair, half):
        head = pair * 2 + half
        rows = pl.ds(pl.multiple_of(head * HD, HD), HD)
        key_rows = pl.ds(pl.multiple_of(D + head * HD, HD), HD)
        lanes = pl.ds(pl.multiple_of(pair * 2 * HD, 2 * HD), 2 * HD)
        query = qtok_s[image_rows(image), lanes][:, half * HD : (half + 1) * HD]
        key = qk_s[key_rows, image_rows(image)]
        value = v_s[rows, image_rows(image)]
        exp_scores = jnp.exp(dot_nn(query, key) - scal_ref[head])
        probs = exp_scores * (1.0 / jnp.sum(exp_scores, axis=-1, keepdims=True))
        return head, rows, key_rows, lanes, key, value, probs

    @pl.loop(0, HEADS // 2)
    def _(pair):
        for image in range(images):
            mixed = []
            for half in range(2):
                _, _, _, lanes, _, value, probs = pair_parts(image, pair, half)
                mixed.append(dot_nt(probs.astype(BF16), value))
            o_s[image_rows(image), lanes] = jnp.concatenate(mixed, axis=1).astype(BF16)

    weights_here(2)
    x2_s[...] = x_ref[...] + dot_nn(o_s[...], w[ROW_O : ROW_O + D])
    for image in range(images):
        x2 = x2_s[image_rows(image)]
        inverse = lax.rsqrt(jnp.mean(x2 * x2, axis=-1, keepdims=True) + NORM_EPS)
        n2_s[image_rows(image)] = (x2 * inverse * gain_two[image : image + 1]).astype(BF16)
    send(n2_s, n2_hbm)

    weights_here(3)
    chunks = FF // CHUNK

    def deal(field, store, place):
        dealt = dot_nt(deal_ref[...], field).astype(BF16)
        store[0, place] = dealt[:HALF_CHUNK]
        store[1, place] = dealt[HALF_CHUNK:]

    @pl.loop(0, chunks)
    def _(chunk):
        def part(base):
            return w[pl.ds(pl.multiple_of(base + chunk * CHUNK, CHUNK), CHUNK)]

        gate = dot_nt(n2_s[...], part(ROW_G))
        up = dot_nt(n2_s[...], part(ROW_U))
        grad_hidden = dot_nt(gb_s[...], part(ROW_F))
        phi_sum = 0.5 * (1.0 + lax.erf(gate * ROOT_HALF))
        density = INV_ROOT_TWO_PI * jnp.exp(-0.5 * gate * gate)
        gelu = gate * phi_sum
        hidden = (gelu * up).astype(BF16)
        grad_gate = (grad_hidden * up * (phi_sum + gate * density)).astype(BF16)
        grad_up = (grad_hidden * gelu).astype(BF16)
        ff = dot_nn(hidden, part(ROW_F))
        dn2 = dot_nn(grad_gate, part(ROW_G)) + dot_nn(grad_up, part(ROW_U))

        @pl.when(chunk == 0)
        def _():
            ff_s[...] = ff
            dn2_s[...] = dn2

        @pl.when(chunk > 0)
        def _():
            ff_s[...] += ff
            dn2_s[...] += dn2

        deal(hidden, hid_s, chunk)
        deal(grad_gate, gu_s, chunk)
        deal(grad_up, gu_s, chunks + chunk)

    send(hid_s.at[0], hid_keep)
    send(hid_s.at[1], hid_send)
    send(gu_s.at[0], gu_keep)
    send(gu_s.at[1], gu_send)
    out_s[...] = (x2_s[...] + ff_s[...]).astype(BF16)
    send(out_s, out_hbm)

    def norm_back(x, gain, grad_normed):
        inverse = lax.rsqrt(jnp.mean(x * x, axis=-1, keepdims=True) + NORM_EPS)
        scaled = grad_normed * gain
        inner = jnp.mean(x * scaled, axis=-1, keepdims=True)
        grad_x = inverse * scaled - x * (inverse * inverse * inverse * inner)
        return grad_x, jnp.sum(grad_normed * x * inverse, axis=0, keepdims=True)

    for image in range(images):
        rows = image_rows(image)
        grad_x, grad_gain = norm_back(x2_s[rows], gain_two[image : image + 1], dn2_s[rows])
        grad = cot_ref[rows].astype(F32) * scal_ref[2 * HEADS + image] + grad_x
        x2_s[rows] = grad
        ga_s[rows] = grad.astype(BF16)
        gain_s[pl.ds(images + image, 1)] = grad_gain
    send(ga_s, ga_hbm)

    do_s[...] = dot_nt(ga_s[...], w[ROW_O : ROW_O + D]).astype(BF16)
    dot_s[...] = dot_nt(w[ROW_O : ROW_O + D], ga_s[...]).astype(BF16)
    ds_s[...] = jnp.zeros_like(ds_s)

    @pl.loop(0, HEADS // 2)
    def _(pair):
        for image in range(images):
            cols = image_rows(image)
            for half in range(2):
                head, rows, key_rows, lanes, key, value, probs = pair_parts(image, pair, half)
                grad_mixed = do_s[cols, lanes][:, half * HD : (half + 1) * HD]
                grad_probs = dot_nn(grad_mixed, value)
                inner = jnp.sum(probs * grad_probs, axis=-1, keepdims=True)
                grad_scores = (probs * (grad_probs - inner)).astype(BF16)
                grad_query = dot_nt(key, grad_scores)
                grad_key = dot_nn(qk_s[rows, cols], grad_scores)
                grad_value = dot_nn(dot_s[rows, cols], probs.astype(BF16))
                angle_rows = pl.ds(pl.multiple_of(head * 16, 16), 16)
                cosine, sine = cos_ref[angle_rows, cols], sin_ref[angle_rows, cols]
                along = jnp.zeros((1, SEQ), F32)
                for grad, own_rows, place in (
                    (grad_query, rows, head),
                    (grad_key, key_rows, HEADS + head),
                ):
                    first, second = grad[:16], grad[16:32]
                    back = jnp.concatenate(
                        [
                            first * cosine + second * sine,
                            second * cosine - first * sine,
                            grad[32:],
                        ],
                        axis=0,
                    )
                    unit = unit_s[own_rows, cols]
                    inner_unit = jnp.sum(unit * back, axis=0, keepdims=True)
                    along += inner_unit
                    dqkv_s[own_rows, cols] = (
                        coef_s[pl.ds(place, 1), cols] * (back - unit * inner_unit)
                    ).astype(BF16)
                value_rows = pl.ds(pl.multiple_of(2 * D + head * HD, HD), HD)
                dqkv_s[value_rows, cols] = grad_value.astype(BF16)
                ds_s[pl.ds(head, 1)] += along

    for place in range(2):
        deal(o_s[:, place * CHUNK : (place + 1) * CHUNK], at_s, place)
    for place in range(6):
        dealt = dot_nn(deal_ref[...], dqkv_s[place * CHUNK : (place + 1) * CHUNK]).astype(BF16)
        at_s[0, 2 + place] = dealt[:HALF_CHUNK]
        at_s[1, 2 + place] = dealt[HALF_CHUNK:]
    send(at_s.at[0], at_keep)
    send(at_s.at[1], at_send)
    dsout_s[...] = jnp.broadcast_to(jnp.sum(ds_s[...], axis=1, keepdims=True), dsout_s.shape)
    send(dsout_s, ds_hbm)

    dn1 = dot_nn(dqkv_s[:D].T, w[ROW_Q : ROW_Q + D])
    dn1 += dot_nn(dqkv_s[D : 2 * D].T, w[ROW_K : ROW_K + D])
    dn1 += dot_nn(dqkv_s[2 * D :].T, w[ROW_V : ROW_V + D])
    dn2_s[...] = dn1
    for image in range(images):
        rows = image_rows(image)
        grad_x, grad_gain = norm_back(x_ref[rows], gain_one[image : image + 1], dn2_s[rows])
        gin_s[rows] = (x2_s[rows] + grad_x).astype(BF16)
        gain_s[pl.ds(image, 1)] = grad_gain
    send(gin_s, grad_hbm)
    send(gain_s, gain_hbm)
    for copy in sends:
        copy.wait()


def run_layer(images, source, scalars, x, cotangent, cond, cosine, sine, deal, slots):
    toks = images * SEQ
    chunks = FF // CHUNK
    any_spec = pl.BlockSpec(memory_space=pl.ANY)
    vmem = pl.BlockSpec(memory_space=pltpu.VMEM)
    smem = pl.BlockSpec(memory_space=pltpu.SMEM)
    field = jax.ShapeDtypeStruct((toks, D), BF16)

    def dealt(count):
        return jax.ShapeDtypeStruct((count, HALF_CHUNK, toks), BF16)

    outs = [field, field]
    outs += [dealt(chunks)] * 2 + [dealt(2 * chunks)] * 2 + [dealt(8)] * 2
    outs += [field] * 4
    outs += [
        jax.ShapeDtypeStruct((2 * images, D), F32),
        jax.ShapeDtypeStruct((16, 128), F32),
    ]
    wide = pltpu.VMEM((toks, D), F32)
    low = pltpu.VMEM((toks, D), BF16)
    scratch = [
        pltpu.VMEM((ROWS_ALL, D), BF16),
        pltpu.VMEM((2 * D, toks), F32),
        pltpu.VMEM((2 * HEADS, toks), F32),
        low,
        pltpu.VMEM((2 * D, toks), BF16),
        pltpu.VMEM((D, toks), BF16),
        low,
        wide,
        low,
        low,
        low,
        low,
        low,
        pltpu.VMEM((D, toks), BF16),
        wide,
        wide,
        pltpu.VMEM((3 * D, toks), BF16),
        pltpu.VMEM((2, chunks, HALF_CHUNK, toks), BF16),
        pltpu.VMEM((2, 2 * chunks, HALF_CHUNK, toks), BF16),
        pltpu.VMEM((2, 8, HALF_CHUNK, toks), BF16),
        low,
        low,
        pltpu.VMEM((2 * images, D), F32),
        pltpu.VMEM((16, SEQ), F32),
        pltpu.VMEM((16, 128), F32),
        pltpu.SemaphoreType.DMA((4,)),
        pltpu.SemaphoreType.DMA((16,)),
    ]

    def body(*refs):
        layer_kernel(images, *refs)

    return pl.pallas_call(
        body,
        out_shape=outs,
        in_specs=[smem, smem] + [vmem] * 6 + [any_spec],
        out_specs=[any_spec] * len(outs),
        scratch_shapes=scratch,
        compiler_params=pltpu.CompilerParams(vmem_limit_bytes=VMEM_BYTES),
        cost_estimate=pl.CostEstimate(
            flops=2 * 3 * ROWS_ALL * D * toks, bytes_accessed=ROWS_ALL * D * 4, transcendentals=0
        ),
        name="layer",
    )(source, scalars, x, cotangent, cond, cosine, sine, deal, slots)


def weight_grads(groups, halves):
    rows, toks = groups[0][0][0].shape[1:]
    pieces = rows // (2 * SPAN)
    operands, specs, places, flops, moved = [], [], [], 0, 0
    total = 0
    for lefts, rights, first, here in groups:
        assert first % here == 0
        places.append((len(lefts), len(operands), total, here))
        total += here
        for left in lefts:
            operands.append(left)
            specs.append(
                pl.BlockSpec((here, rows, toks), lambda half, at=first // here: (at + half, 0, 0))
            )
        for right in rights:
            operands.append(right)
            specs.append(pl.BlockSpec((toks, D), lambda half: (0, 0)))
        flops += 2 * len(lefts) * here * halves * rows * toks * D
        moved += len(lefts) * 2 * (here * halves * rows * toks + toks * D)

    def body(*refs):
        out_ref = refs[-1]
        for count, start, at, here in places:
            lefts, rights = refs[start : start + count], refs[start + count : start + 2 * count]
            summed = dot_nn(lefts[0][...].reshape(here * rows, toks), rights[0][...])
            for left, right in zip(lefts[1:], rights[1:]):
                summed += dot_nn(left[...].reshape(here * rows, toks), right[...])
            for chunk in range(here):
                out_ref[0, :, at + chunk] = (
                    summed[chunk * rows : (chunk + 1) * rows]
                    .reshape(pieces, 2 * SPAN, D)
                    .astype(BF16)
                )

    return pl.pallas_call(
        body,
        out_shape=jax.ShapeDtypeStruct((halves, pieces, total, 2 * SPAN, D), BF16),
        grid=(halves,),
        in_specs=specs,
        out_specs=pl.BlockSpec(
            (1, pieces, total, 2 * SPAN, D), lambda half: (half, 0, 0, 0, 0)
        ),
        compiler_params=pltpu.CompilerParams(vmem_limit_bytes=VMEM_BYTES),
        cost_estimate=pl.CostEstimate(
            flops=flops,
            bytes_accessed=moved + halves * pieces * total * 4 * SPAN * D,
            transcendentals=0,
        ),
        name="weight_grads",
    )(*operands)


def adam_step(weights, first_new, second_new, rate):
    fix_one = 1.0 - math.pow(BETA_ONE, STEP)
    fix_two = 1.0 - math.pow(BETA_TWO, STEP)
    return weights * (1.0 - rate * WEIGHT_DECAY) - rate * (first_new / fix_one) / (
        jnp.sqrt(second_new / fix_two) + ADAM_EPS
    )


def add(*terms):
    total = terms[0].astype(F32)
    for term in terms[1:]:
        total = total + term.astype(F32)
    return total


class Ring:
    def __init__(self, dp_count):
        self.count = dp_count // 2
        pairs = []
        for place in range(self.count):
            for core in range(2):
                pairs.append(
                    (self.chip(place) * 2 + core, self.chip((place + 1) % self.count) * 2 + core)
                )
        self.onward = pairs
        self.backward = [(b, a) for a, b in pairs]
        self.twins = [(index, index ^ 1) for index in range(dp_count)]

    def chip(self, place):
        column = self.count // 2
        return 2 * place if place < column else 2 * (self.count - 1 - place) + 1

    def here(self):
        chip = lax.axis_index("dp") // 2
        return jnp.where(chip % 2 == 0, chip // 2, self.count - 1 - chip // 2)

    def chip_at(self, offset):
        place = (self.here() + offset + self.count) % self.count
        column = self.count // 2
        return jnp.where(place < column, 2 * place, 2 * (self.count - 1 - place) + 1)

    def on(self, field):
        return lax.ppermute(field, "dp", self.onward)

    def back(self, field):
        return lax.ppermute(field, "dp", self.backward)

    def twin(self, field):
        return lax.ppermute(field, "dp", self.twins)


def after(field, *others):
    return lax.optimization_barrier((field, *others))[0]


def swap_mp(field):
    return lax.ppermute(field, "mp", [(0, 1), (1, 0)])


def both_halves(own, other, half):
    return jnp.where(
        half == 0, jnp.concatenate([own, other]), jnp.concatenate([other, own])
    )


def pick(field, *places):
    for place in places:
        field = lax.dynamic_index_in_dim(field, place, 0, keepdims=False)
    return field


def reduce_ring_first(ring, field, half, beside):
    far = ring.count // 2

    def block(offset):
        return lax.dynamic_index_in_dim(field, ring.chip_at(offset), 1, keepdims=False)

    far_block = block(far)
    on = ring.on(far_block[0])
    back = ring.back(far_block[1])
    own = block(far - 1)
    on = ring.on(jnp.stack([add(own[0], on).astype(BF16), own[1]]))
    own = block(1 - far)
    back = ring.back(jnp.stack([own[0], add(own[1], back).astype(BF16)]))
    for distance in range(far - 2, 0, -1):
        if distance == 1:
            on = after(on, beside)
        on = ring.on(add(block(distance), on).astype(BF16))
        back = ring.back(add(block(-distance), back).astype(BF16))
    total = add(block(0), on, back)
    other = swap_mp(pick(total.astype(BF16), 1 - half))
    return add(pick(total, half), other)


def gather_small(field, dp_count):
    step = dp_count // 2
    while step > 1:
        other = lax.ppermute(field, "dp", [(i, i ^ step) for i in range(dp_count)])
        field = jnp.concatenate([field, other])
        step //= 2
    field = jnp.concatenate([field, swap_mp(field)])
    other = lax.ppermute(field, "dp", [(i, i ^ 1) for i in range(dp_count)])
    return jnp.concatenate([field, other])


def on_device(
    tokens,
    conditioning,
    sigmas,
    positions,
    cotangent,
    owners,
    master,
    moment_one,
    moment_two,
    scale_state,
):
    dp_count = lax.axis_size("dp")
    mp_count = lax.axis_size("mp")
    dp_index = lax.axis_index("dp")
    mp_index = lax.axis_index("mp")
    images = conditioning.shape[0] // mp_count
    toks = images * SEQ
    slots = master.shape[1]
    unit_rows = master.shape[2]
    unit_count = owners.shape[1]
    heads_here = scale_state.shape[1]
    paired = dp_count * 2 == UNIT
    core = dp_index % 2 if paired else 0

    def mine(field, rows):
        return lax.dynamic_slice_in_dim(field, mp_index * rows, rows, 0)

    rounded = master[0].astype(BF16)
    gathered = lax.all_gather(rounded, ("dp", "mp"), axis=0, tiled=True)
    halves_here = jnp.concatenate([owners[0].astype(F32), scale_state[0]])
    halves_all = both_halves(halves_here[None], swap_mp(halves_here[None]), mp_index)
    owners_all = halves_all[:, :unit_count].astype(jnp.int32)
    scales_all = halves_all[:, unit_count:].reshape(-1)
    before = jnp.stack([slots_before(owners_all[half]) for half in range(mp_count)])
    half_ids = lax.broadcasted_iota(jnp.int32, owners_all.shape, 0)
    place = (owners_all * mp_count + half_ids) * slots + before
    by_chunk = place.reshape(mp_count, -1, SPAN)
    order = {}
    for chunk, kind in enumerate(STACK_ORDER):
        order.setdefault(kind, []).append(chunk)
    source = jnp.concatenate(
        [
            by_chunk[:, order[kind][0] : order[kind][-1] + 1].reshape(-1)
            for kind in ("A1", "A2", "Q", "K", "V", "O", "G", "U", "F")
        ]
    )
    square = sigmas * sigmas
    data_square = SIGMA_DATA * SIGMA_DATA
    loss_weight = 4.0 * square * data_square / ((square + data_square) * (square + data_square))
    scalars = jnp.concatenate([scales_all, jnp.sqrt(scales_all), mine(loss_weight, images)])
    cosine, sine = rope_tables(mine(positions, images))
    cond = jnp.pad(mine(conditioning, images).astype(BF16), ((0, 16 - images), (0, 0)))

    (
        out_low,
        grad_low,
        hid_keep,
        hid_send,
        gu_keep,
        gu_send,
        at_keep,
        at_send,
        normed_one,
        normed_two,
        grad_out,
        grad_mid,
        grad_gains,
        grad_scale,
    ) = run_layer(
        images,
        source,
        scalars,
        mine(tokens, toks),
        mine(cotangent, toks),
        cond,
        cosine,
        sine,
        deal_matrix(core),
        gathered,
    )

    out_other = swap_mp(out_low)
    grad_other = swap_mp(grad_low)
    output = both_halves(out_low, out_other, mp_index).astype(F32)
    input_grad = both_halves(grad_low, grad_other, mp_index).astype(F32)

    def small_factors(*before_it):
        cond_own = mine(conditioning, images).astype(BF16).astype(F32)
        scale_row = jnp.pad(grad_scale[:, 0], (0, D - 16))[None]
        own = jnp.concatenate([cond_own, grad_gains, scale_row, jnp.zeros((1, D), F32)], axis=0)
        small = gather_small(after(own, *before_it), dp_count).reshape(-1, 3 * images + 2, D)
        scale_sum = jnp.sum(small[:, 3 * images, :HEADS], axis=0) / (2.0 * jnp.sqrt(scales_all))
        gains = [
            small[:, place * images : (place + 1) * images].reshape(-1, D) for place in (1, 2)
        ]
        return (
            small[:, :images].reshape(-1, D),
            jnp.concatenate(gains, axis=1),
            lax.dynamic_slice_in_dim(scale_sum, mp_index * heads_here, heads_here, 0),
        )

    if paired:
        ring = Ring(dp_count)
        chunks = FF // CHUNK
        here = chunks // mp_count
        hid_both = (hid_keep, ring.twin(hid_send))
        out_both = (grad_out, ring.twin(grad_out))
        gu_both = (gu_keep, ring.twin(gu_send))
        two_both = (normed_two, ring.twin(normed_two))
        at_both = (at_keep, ring.twin(at_send))
        mid_both = (grad_mid, ring.twin(grad_mid))
        one_both = (normed_one, ring.twin(normed_one))
        grad_fg = weight_grads(
            ((hid_both, out_both, 0, here), (gu_both, two_both, 0, here)), mp_count
        )
        grad_rest = weight_grads(
            (
                (gu_both, two_both, chunks, here),
                (at_both, mid_both, 0, 1),
                (at_both, one_both, mp_count, 1),
                (at_both, one_both, 2 * mp_count, 1),
                (at_both, one_both, 3 * mp_count, 1),
            ),
            mp_count,
        )
        cond_all, gains_all, scale_grad = small_factors(grad_fg, grad_rest)
        sum_fg = reduce_ring_first(ring, grad_fg, mp_index, out_other)
        sum_rest = reduce_ring_first(ring, grad_rest, mp_index, grad_other)
        wanted = lax.broadcasted_iota(jnp.int32, (2 * SPAN, D), 0)
        feature = lax.broadcasted_iota(jnp.int32, (2 * SPAN, D), 1)
        wanted = (mp_index * SPAN + wanted % SPAN) * UNIT + 2 * dp_index + wanted // SPAN
        cond_rows = dot_nt((feature == wanted).astype(F32), cond_all)
        sum_a = jnp.dot(
            cond_rows,
            gains_all,
            precision=lax.Precision.HIGHEST,
            preferred_element_type=F32,
        )
        by_kind = jnp.concatenate(
            [
                sum_a[None, :, :D],
                sum_rest[here + 1 :],
                sum_rest[here : here + 1],
                sum_a[None, :, D:],
                sum_fg[here:],
                sum_rest[:here],
                sum_fg[:here],
            ]
        )
        grad_shards = (
            by_kind.reshape(-1, 2, SPAN, D).transpose(0, 2, 1, 3).reshape(unit_count, 2 * D)
        )
    else:
        def units_of(parts, field, kinds):
            here = parts[0].shape[0] // (kinds * mp_count)
            sides = jnp.stack(
                [
                    jnp.concatenate(
                        [
                            weight_grads(
                                (((part,), (field,), kind * mp_count * here, here),), mp_count
                            )
                            for kind in range(kinds)
                        ],
                        axis=2,
                    )
                    for part in parts
                ]
            )
            sides = sides.reshape(2, mp_count, UNIT // 4, -1, 2, SPAN, D)
            return sides.transpose(1, 3, 5, 2, 0, 4, 6).reshape(mp_count, -1, unit_rows * D)

        summed = lax.psum_scatter(
            jnp.concatenate(
                [
                    units_of((at_keep[2:], at_send[2:]), normed_one, 3),
                    units_of((at_keep[:2], at_send[:2]), grad_mid, 1),
                    units_of((gu_keep, gu_send), normed_two, 2),
                    units_of((hid_keep, hid_send), grad_out, 1),
                ],
                axis=1,
            ),
            "mp",
            scatter_dimension=0,
            tiled=True,
        )[0]
        summed = lax.psum_scatter(summed, "dp", scatter_dimension=1, tiled=True).astype(F32)
        cond_all, gains_all, scale_grad = small_factors()
        cond_half = lax.dynamic_slice_in_dim(
            cond_all, mp_index * SPAN * unit_rows, SPAN * unit_rows, 1
        )
        sum_a = lax.dot_general(
            cond_half,
            gains_all,
            (((0,), (0,)), ((), ())),
            precision=lax.Precision.HIGHEST,
            preferred_element_type=F32,
        )
        width = unit_rows * D // dp_count

        def piece(field):
            return lax.dynamic_slice_in_dim(
                field.reshape(SPAN, unit_rows * D), dp_index * width, width, 1
            )

        grad_shards = jnp.concatenate(
            [
                piece(sum_a[:, :D]),
                summed[: 4 * SPAN],
                piece(sum_a[:, D:]),
                summed[4 * SPAN :],
            ]
        )

    placed = owners[0] * slots + slots_before(owners[0])
    total_slots = dp_count * slots
    slot_ids = lax.broadcasted_iota(jnp.int32, (total_slots, unit_count), 0)
    unit_ids = lax.broadcasted_iota(jnp.int32, (total_slots, unit_count), 1)
    match_table = slot_ids == placed[None, :]
    source_unit = jnp.sum(jnp.where(match_table, unit_ids, 0), axis=1)
    filled = jnp.any(match_table, axis=1)
    outgoing = jnp.where(
        filled[:, None], jnp.take(grad_shards.astype(BF16), source_unit, axis=0), 0.0
    )
    owned = lax.all_to_all(outgoing, "dp", split_axis=0, concat_axis=1, tiled=True)
    owned_grads = owned.reshape(slots, unit_rows, D).astype(F32)
    first_new = BETA_ONE * moment_one[0] + (1.0 - BETA_ONE) * owned_grads
    second_new = BETA_TWO * moment_two[0] + (1.0 - BETA_TWO) * owned_grads * owned_grads
    master_new = adam_step(master[0], first_new, second_new, LEARN_RATE)
    scale_first = BETA_ONE * scale_state[1] + (1.0 - BETA_ONE) * scale_grad
    scale_second = BETA_TWO * scale_state[2] + (1.0 - BETA_TWO) * scale_grad * scale_grad
    scale_new = adam_step(scale_state[0], scale_first, scale_second, SCALE_RATE)
    scale_update = jnp.stack([scale_first, scale_new])
    return (
        output,
        input_grad,
        grad_shards[None],
        master_new[None],
        first_new[None],
        second_new[None],
        scale_update,
        scale_second,
    )


def solution(mesh):
    in_specs = (
        P("dp", None),
        P("dp", None),
        P("dp"),
        P("dp", None, None),
        P("dp", None),
        P("mp", None),
        P("mp", "dp", None, None),
        P("mp", "dp", None, None),
        P("mp", "dp", None, None),
        P(None, "mp"),
    )
    out_specs = (
        P("dp", None),
        P("dp", None),
        P("mp", None, "dp"),
        P("mp", "dp", None, None),
        P("mp", "dp", None, None),
        P("mp", "dp", None, None),
        P(None, "mp"),
        P("mp"),
    )
    return jax.shard_map(
        on_device, mesh=mesh, in_specs=in_specs, out_specs=out_specs, check_vma=False
    )
```

time: 922 us -> 370 us (0.40)
  waiting for transfers between devices: 549 us -> 179 us
  local copies, waits for them, and re-layouts: 138 us -> 21.2 us
  matrix products: 77.8 us -> 0.51 us
  Pallas kernels: 0 us -> 76 us
  blocking collectives: 63 us -> 0 us
  starting transfers between devices: 12.7 us -> 39.5 us
  other arithmetic: 59.1 us -> 38.9 us
    psum x4 -> x0, waiting for transfers between devices: 265 us -> none  [the longest x1 88.5 us: on_device(): lax.psum(jnp.dot(grad_gu, back_gu, preferred_element_type=jnp.float32), '...]
    reduce_scatter x1 -> x0, waiting for transfers between devices: 188 us -> none  [on_device(): lax.psum_scatter(local_grads, 'dp', scatter_dimension=1, tiled=True)]
    dot_general x23 -> x2, matrix products: 77.8 us -> 0.51 us  [the longest x1 0.32 us: on_device(): jnp.dot(cond_rows, gains_all, precision=lax.Precision.HIGHEST, preferred_...]
    pallas_call x0 -> x3, Pallas kernels: none -> 76 us  [the longest x1 56.5 us: run_layer(): pl.pallas_call(body, out_shape=outs, in_specs=[smem, smem] + [vmem] * 6 +...]
    ppermute x0 -> x33, waiting for transfers between devices: none -> 56.3 us  [the longest x8 26 us: on(): return lax.ppermute(field, 'dp', self.onward)]
    unnamed x1 -> x0, blocking collectives: 53.3 us -> none
    slice x20 -> x12, local copies, waits for them, and re-layouts: 45.5 us -> 1.23 us  [the longest x1 0.81 us: small_factors(): scale_row = jnp.pad(grad_scale[:, 0], (0, D - 16))[None]]
    all_gather x1, waiting for transfers between devices: 78.2 us -> 116 us  [on_device(): gathered = lax.all_gather(rounded, ('dp', 'mp'), axis=0, tiled=True)]
  transfers between devices with their start and end apart: 8 -> 35, of which waited for: 7 -> 17; matrix products, arithmetic and copies ran while one was open for 6% -> 12% of each run, Pallas kernels for 0% -> 5%
where the time goes in v1:
time: 370 us
  waiting for transfers between devices  179 us (48%)
  Pallas kernels  76 us (21%)
  starting transfers between devices  39.5 us (11%)
  other arithmetic  38.9 us (11%)
  local copies, waits for them, and re-layouts  21.2 us (6%)
  between operations  14.7 us (4%)
    all_gather x1, waiting for transfers between devices, on_device(): gathered = lax.all_gather(rounded, ('dp', 'mp'), axis=0, tiled=True)  116 us
    pallas_call x1, Pallas kernels, run_layer(): pl.pallas_call(body, out_shape=outs, in_specs=[smem, smem] + [vmem] * 6 +...  56.5 us
    ppermute x8, waiting for transfers between devices, on(): return lax.ppermute(field, 'dp', self.onward)  26 us
    pallas_call x2, Pallas kernels, weight_grads(): pl.pallas_call(body, out_shape=jax.ShapeDtypeStruct((halves, pieces, tota...  19.5 us
    ppermute x6, starting transfers between devices, swap_mp(): return lax.ppermute(field, 'mp', [(0, 1), (1, 0)])  10.4 us
    ppermute x3, waiting for transfers between devices, gather_small(): other = lax.ppermute(field, 'dp', [(i, i ^ step) for i in range(dp_count)])  9.79 us
    ppermute x8, starting transfers between devices, back(): return lax.ppermute(field, 'dp', self.backward)  9.52 us
    ppermute x8, waiting for transfers between devices, back(): return lax.ppermute(field, 'dp', self.backward)  9.5 us
  transfers between devices with their start and end apart: 35, of which 17 were waited for; matrix products, arithmetic and copies ran while one was open for 12% of the time, Pallas kernels for 5%

profile of v1, /device:TPU:0, one launch (start us, length us, event | category | flops | bytes accessed | tf_op | source)
XLA Modules:
  0.0 369.7 jit_solution(9458434381282668225)
XLA Ops:
  7.3 2.3 bitcast_convert_fusion
  9.7 3.0 collective-permute-start
  23.2 115.8 %all-gather.3.cloned.1.call-done = bf16[1,384,32,768]{3,2,0,1:T(8,128)(2,1)} async-done(((bf16[1,12,32,768]{3,2,0,1:T(8,128)(2,1)}), bf16[1,384,32,768]{3,2,0,1:T(8,128)(2,1)}) %all-gather.3.cloned.1.call-update) | async-done | bytes 18874384 | tf_op jit(solution)/shard_map/all_gather | solution.py:618
  139.1 56.5 %layer.1 = (bf16[512,768]{1,0:T(8,128)(2,1)}, bf16[512,768]{1,0:T(8,128)(2,1)}, bf16[6,192,512]{2,1,0:T(8,128)(2,1)}, bf16[6,192,512]{2,1,0:T(8,128)(2,1)}, bf16...) custom-call(s32[360]{0:T(512)} %concatenate.76.refs_0_, ...), custom_call_target="tpu_custom_call" | custom-call | flops 27179089920 | bytes 35389440 | tf_op jit(solution)/shard_map/layer/pallas_call | solution.py:418
  197.9 4.7 %collective-permute-done.6.refs_7_.refs_3_ = bf16[512,768]{1,0:T(8,128)(2,1)S(1)} collective-permute-done((bf16[512,768]{1,0:T(8,128)(2,1)}, bf16[512,768]{1,0:T(8,128)(2,1)S(1)}, u32[]{:S(2)}, u32[]{:S(2)}) %collective-permute-start.6) | collective-permute-done | bytes 786464 | tf_op jit(solution)/shard_map/ppermute | solution.py:532
  209.1 8.0 %weight_grads.2 = bf16[2,8,6,24,768]{4,3,2,1,0:T(8,128)(2,1)} custom-call(bf16[6,192,512]{2,1,0:T(8,128)(2,1)} %get-tuple-element.29.refs_0_, bf16[6,192,512]{2,1,0:T(8,128)(2,1)} %collective-permute-done.3.refs_1_, bf16[512,768]{1,0:T(8,128)(2,1)} %get-tuple-element.31.refs_2_, bf16[512,768]{1,0:T(8,128)(2,1)} %copy-done.6, ...), custom_call_target="tpu_custom_call" | custom-call | flops 3623878656 | bytes 11403264 | tf_op jit(solution)/shard_map/weight_grads/pallas_call | solution.py:466
  220.9 11.5 %weight_grads.3 = bf16[2,8,7,24,768]{4,3,2,1,0:T(8,128)(2,1)} custom-call(bf16[12,192,512]{2,1,0:T(8,128)(2,1)} %get-tuple-element.32.refs_4_.refs_0_, bf16[12,192,512]{2,1,0:T(8,128)(2,1)} %collective-permute-done.5.refs_5_.refs_1_, bf16[512,768]{1,0:T(8,128)(2,1)} %get-tuple-element.34.refs_6_.refs_2_, bf16[512,768]{1,0:T(8,128)(2,1)} %copy-done.4, ...), custom_call_target="tpu_custom_call" | custom-call | flops 4227858432 | bytes 17498112 | tf_op jit(solution)/shard_map/weight_grads/pallas_call | solution.py:466
  238.7 5.1 %collective-permute-done.11 = f32[16,768]{1,0:T(8,128)S(1)} collective-permute-done((f32[16,768]{1,0:T(8,128)S(1)}, f32[16,768]{1,0:T(8,128)S(1)}, u32[]{:S(2)}, u32[]{:S(2)}) %collective-permute-start.11) | collective-permute-done | bytes 49184 | tf_op jit(solution)/shard_map/ppermute | solution.py:581
  245.1 3.4 collective-permute-done.12
  260.1 5.1 %collective-permute-done.29 = bf16[2,6,24,768]{3,2,1,0:T(8,128)(2,1)S(1)} collective-permute-done((bf16[2,6,24,768]{3,2,1,0:T(8,128)(2,1)S(1)}, bf16[2,6,24,768]{3,2,1,0:T(8,128)(2,1)S(1)}, u32[]{:S(2)}, u32[]{:S(2)}) %collective-permute-start.29) | collective-permute-done | bytes 442400 | tf_op jit(solution)/shard_map/ppermute | solution.py:529
  269.6 2.7 collective-permute-start.26
  273.8 3.1 collective-permute-done.20
  278.2 3.0 collective-permute-done.16
  285.9 4.9 %collective-permute-done.26 = bf16[2,6,24,768]{3,2,1,0:T(8,128)(2,1)} collective-permute-done((bf16[2,6,24,768]{3,2,1,0:T(8,128)(2,1)}, bf16[2,6,24,768]{3,2,1,0:T(8,128)(2,1)}, u32[]{:S(2)}, u32[]{:S(2)}) %collective-permute-start.26) | collective-permute-done | bytes 442400 | tf_op jit(solution)/shard_map/ppermute | solution.py:526
  294.5 7.2 %collective-permute-done.17 = bf16[2,7,24,768]{3,2,1,0:T(8,128)(2,1)S(1)} collective-permute-done((bf16[2,7,24,768]{3,2,1,0:T(8,128)(2,1)}, bf16[2,7,24,768]{3,2,1,0:T(8,128)(2,1)S(1)}, u32[]{:S(2)}, u32[]{:S(2)}) %collective-permute-start.17) | collective-permute-done | bytes 516128 | tf_op jit(solution)/shard_map/ppermute | solution.py:526
  305.3 5.9 %collective-permute-done.27 = bf16[2,6,24,768]{3,2,1,0:T(8,128)(2,1)S(1)} collective-permute-done((bf16[2,6,24,768]{3,2,1,0:T(8,128)(2,1)S(1)}, bf16[2,6,24,768]{3,2,1,0:T(8,128)(2,1)S(1)}, u32[]{:S(2)}, u32[]{:S(2)}) %collective-permute-start.27) | collective-permute-done | bytes 442400 | tf_op jit(solution)/shard_map/ppermute | solution.py:526
  314.7 3.5 collective-permute-done.18
  322.0 4.8 %collective-permute-done.23 = bf16[7,24,768]{2,1,0:T(8,128)(2,1)} collective-permute-done((bf16[7,24,768]{2,1,0:T(8,128)(2,1)}, bf16[7,24,768]{2,1,0:T(8,128)(2,1)}, u32[]{:S(2)}, u32[]{:S(2)}) %collective-permute-start.23) | collective-permute-done | bytes 258080 | tf_op jit(solution)/shard_map/ppermute | solution.py:540
  332.1 5.1 %all-to-all-start = ((bf16[16,12,1536]{2,1,0:T(8,128)(2,1)}), bf16[16,12,1536]{2,1,0:T(8,128)(2,1)S(1)}, u32[]{:S(2)}, u32[]{:S(2)}) async-start(bf16[16,12,1536]{2,1,0:T(8,128)(2,1)} %select_select_fusion), calls=%async_computation | async-start | bytes 1572864 | tf_op jit(solution)/shard_map/all_to_all | solution.py:814
  337.2 3.9 %fusion.1 = f32[1024,768]{1,0:T(8,128)} fusion(bf16[512,768]{1,0:T(8,128)(2,1)} %collective-permute-done.2, bf16[512,768]{1,0:T(8,128)(2,1)} %get-tuple-element.26, pred[]{:T(512)S(6)} %eq.123), kind=kLoop, calls=%fused_computation.11 | loop fusion | flops 7864320 | bytes 4718593 | tf_op jit(solution)/shard_map/convert_element_type | solution.py:674
  341.1 3.3 fusion
  346.6 2.6 broadcast_in_dim_reshape.4
  349.2 6.7 %all-to-all-done = bf16[16,12,1536]{2,1,0:T(8,128)(2,1)S(1)} async-done(((bf16[16,12,1536]{2,1,0:T(8,128)(2,1)}), bf16[16,12,1536]{2,1,0:T(8,128)(2,1)S(1)}, u32[]{:S(2)}, u32[]{:S(2)}) %all-to-all-start) | async-done | bytes 589856 | tf_op jit(solution)/shard_map/all_to_all | solution.py:814
  358.0 4.8 %divide_subtract_fusion = (f32[1,12,32,768]{3,2,1,0:T(8,128)}, f32[1,12,32,768]{3,2,1,0:T(8,128)}, f32[1,12,32,768]{3,2,1,0:T(8,128)}) fusion(f32[1,12,32,768]{3,2,1,0:T(8,128)} %param.16, f32[1,12,32,768]{3,2,1,0:T(8,128)} %reshape.239, f32[1,12,32,768]{3,2,1,0:T(8,128)} %param.17, f32[1,12,32,768]{3,2,1,0:T(8,128)} %param.18), kind=kLoop, calls=%fused_computation.19 | loop fusion | flops 3538944 | bytes 8257536 | tf_op jit(solution)/shard_map/sub | solution.py:487
  (207 shorter events, 78.0 us)
Async XLA Ops:
  7.2 131.8 %all-gather.3.cloned.1.call-start = ((), (), s32[]{:S(2)}) async-start(), calls=%async_computation.1 | async-start | bytes 19464192 | tf_op jit(solution)/shard_map/all_gather | solution.py:618
  9.7 10.8 %collective-permute-start = (f32[1,186]{1,0:T(1,128)S(1)}, f32[1,186]{1,0:T(1,128)S(1)}, u32[]{:S(2)}, u32[]{:S(2)}) collective-permute-start(f32[1,186]{1,0:T(1,128)S(1)} %bitcast.166), channel_id=1, source_target_pairs={{0,1},{1,0},{2,3},{3,2},{4,5},{5,4},{6,7},{7,6},{8,9},{9,8},{10,11... | collective-permute-start | bytes 2240 | tf_op jit(solution)/shard_map/ppermute | solution.py:540
  195.5 13.0 %collective-permute-start.5 = (bf16[12,192,512]{2,1,0:T(8,128)(2,1)}, bf16[12,192,512]{2,1,0:T(8,128)(2,1)}, u32[]{:S(2)}, u32[]{:S(2)}) collective-permute-start(bf16[12,192,512]{2,1,0:T(8,128)(2,1)} %get-tuple-element.33), channel_id=1, source_target_pairs={{0,2},{2,0},{4,6},{6,4},{8,10},{10,8},{12,14},{14,12},{16,18},{18,... | collective-permute-start | bytes 7077896 | tf_op jit(solution)/shard_map/ppermute | solution.py:532
  196.3 10.8 %collective-permute-start.3 = (bf16[6,192,512]{2,1,0:T(8,128)(2,1)}, bf16[6,192,512]{2,1,0:T(8,128)(2,1)}, u32[]{:S(2)}, u32[]{:S(2)}) collective-permute-start(bf16[6,192,512]{2,1,0:T(8,128)(2,1)} %get-tuple-element.30), channel_id=1, source_target_pairs={{0,2},{2,0},{4,6},{6,4},{8,10},{10,8},{12,14},{14,12},{16,18},{18,... | collective-permute-start | bytes 3538952 | tf_op jit(solution)/shard_map/ppermute | solution.py:532
  197.5 21.7 %collective-permute-start.7 = (bf16[8,192,512]{2,1,0:T(8,128)(2,1)}, bf16[8,192,512]{2,1,0:T(8,128)(2,1)S(1)}, u32[]{:S(2)}, u32[]{:S(2)}) collective-permute-start(bf16[8,192,512]{2,1,0:T(8,128)(2,1)} %get-tuple-element.36), channel_id=1, source_target_pairs={{0,2},{2,0},{4,6},{6,4},{8,10},{10,8},{12,14},{14,12},{16,18},{18,... | collective-permute-start | bytes 4718600 | tf_op jit(solution)/shard_map/ppermute | solution.py:532
  202.6 16.6 %collective-permute-start.8 = (bf16[512,768]{1,0:T(8,128)(2,1)}, bf16[512,768]{1,0:T(8,128)(2,1)S(1)}, u32[]{:S(2)}, u32[]{:S(2)}) collective-permute-start(bf16[512,768]{1,0:T(8,128)(2,1)} %get-tuple-element.37.refs_6_), channel_id=1, source_target_pairs={{0,2},{2,0},{4,6},{6,4},{8,10},{10,8},{12,14},{14,12},{16,18},{18,... | collective-permute-start | bytes 2359304 | tf_op jit(solution)/shard_map/ppermute | solution.py:532
  205.2 14.1 %collective-permute-start.9 = (bf16[512,768]{1,0:T(8,128)(2,1)}, bf16[512,768]{1,0:T(8,128)(2,1)S(1)}, u32[]{:S(2)}, u32[]{:S(2)}) collective-permute-start(bf16[512,768]{1,0:T(8,128)(2,1)} %get-tuple-element.38.refs_10_.refs_14_.refs_18_), channel_id=1, source_target_pairs={{0,2},{2,0},{4,6},{6,4},{8,10},{10,8},{12,14},{14,12},{16,18},{18,... | collective-permute-start | bytes 2359304 | tf_op jit(solution)/shard_map/ppermute | solution.py:532
  207.0 77.5 %collective-permute-start.1 = (bf16[512,768]{1,0:T(8,128)(2,1)}, bf16[512,768]{1,0:T(8,128)(2,1)}, u32[]{:S(2)}, u32[]{:S(2)}) collective-permute-start(bf16[512,768]{1,0:T(8,128)(2,1)} %get-tuple-element.25), channel_id=1, source_target_pairs={{0,1},{1,0},{2,3},{3,2},{4,5},{5,4},{6,7},{7,6},{8,9},{9,8},{10,11... | collective-permute-start | bytes 2359304 | tf_op jit(solution)/shard_map/ppermute | solution.py:540
  208.5 86.0 %collective-permute-start.2 = (bf16[512,768]{1,0:T(8,128)(2,1)}, bf16[512,768]{1,0:T(8,128)(2,1)}, u32[]{:S(2)}, u32[]{:S(2)}) collective-permute-start(bf16[512,768]{1,0:T(8,128)(2,1)} %get-tuple-element.26), channel_id=1, source_target_pairs={{0,1},{1,0},{2,3},{3,2},{4,5},{5,4},{6,7},{7,6},{8,9},{9,8},{10,11... | collective-permute-start | bytes 2359304 | tf_op jit(solution)/shard_map/ppermute | solution.py:540
  235.3 13.9 %collective-permute-start.24 = (bf16[6,24,768]{2,1,0:T(8,128)(2,1)}, bf16[6,24,768]{2,1,0:T(8,128)(2,1)S(1)}, u32[]{:S(2)}, u32[]{:S(2)}) collective-permute-start(bf16[6,24,768]{2,1,0:T(8,128)(2,1)} %get-tuple-element.104), channel_id=1, source_target_pairs={{0,8},{2,10},{8,16},{10,18},{16,24},{18,26},{24,28},{26,30},{28,20... | collective-permute-start | bytes 663560 | tf_op jit(solution)/shard_map/ppermute | solution.py:526
  235.8 14.8 %collective-permute-start.28 = (bf16[6,24,768]{2,1,0:T(8,128)(2,1)}, bf16[6,24,768]{2,1,0:T(8,128)(2,1)S(1)}, u32[]{:S(2)}, u32[]{:S(2)}) collective-permute-start(bf16[6,24,768]{2,1,0:T(8,128)(2,1)} %get-tuple-element.107), channel_id=1, source_target_pairs={{8,0},{10,2},{16,8},{18,10},{24,16},{26,18},{28,24},{30,26},{20,28... | collective-permute-start | bytes 663560 | tf_op jit(solution)/shard_map/ppermute | solution.py:529
  254.9 10.3 %collective-permute-start.29 = (bf16[2,6,24,768]{3,2,1,0:T(8,128)(2,1)S(1)}, bf16[2,6,24,768]{3,2,1,0:T(8,128)(2,1)S(1)}, u32[]{:S(2)}, u32[]{:S(2)}) collective-permute-start(bf16[2,6,24,768]{3,2,1,0:T(8,128)(2,1)S(1)} %pad_maximum_fusion.3), channel_id=1, source_target_pairs={{8,0},{10,2},{16,8},{18,10},{24,16},{26,18},{28,24},{30,26},{20,28... | collective-permute-start | bytes 1327112 | tf_op jit(solution)/shard_map/ppermute | solution.py:529
  260.0 9.6 %collective-permute-start.14 = (f32[128,768]{1,0:T(8,128)S(1)}, f32[128,768]{1,0:T(8,128)S(1)}, u32[]{:S(2)}, u32[]{:S(2)}) collective-permute-start(f32[128,768]{1,0:T(8,128)S(1)} %get-tuple-element.116), channel_id=1, source_target_pairs={{0,2},{2,0},{4,6},{6,4},{8,10},{10,8},{12,14},{14,12},{16,18},{18,... | collective-permute-start | bytes 1179656 | tf_op jit(solution)/shard_map/ppermute | solution.py:585
  265.2 11.7 %collective-permute-start.20 = (bf16[2,7,24,768]{3,2,1,0:T(8,128)(2,1)S(1)}, bf16[2,7,24,768]{3,2,1,0:T(8,128)(2,1)S(1)}, u32[]{:S(2)}, u32[]{:S(2)}) collective-permute-start(bf16[2,7,24,768]{3,2,1,0:T(8,128)(2,1)S(1)} %pad_maximum_fusion.1), channel_id=1, source_target_pairs={{8,0},{10,2},{16,8},{18,10},{24,16},{26,18},{28,24},{30,26},{20,28... | collective-permute-start | bytes 1548296 | tf_op jit(solution)/shard_map/ppermute | solution.py:529
  266.5 14.7 %collective-permute-start.16 = (bf16[2,7,24,768]{3,2,1,0:T(8,128)(2,1)S(1)}, bf16[2,7,24,768]{3,2,1,0:T(8,128)(2,1)S(1)}, u32[]{:S(2)}, u32[]{:S(2)}) collective-permute-start(bf16[2,7,24,768]{3,2,1,0:T(8,128)(2,1)S(1)} %pad_maximum_fusion), channel_id=1, source_target_pairs={{0,8},{2,10},{8,16},{10,18},{16,24},{18,26},{24,28},{26,30},{28,20... | collective-permute-start | bytes 1548296 | tf_op jit(solution)/shard_map/ppermute | solution.py:526
  269.6 21.1 %collective-permute-start.26 = (bf16[2,6,24,768]{3,2,1,0:T(8,128)(2,1)}, bf16[2,6,24,768]{3,2,1,0:T(8,128)(2,1)}, u32[]{:S(2)}, u32[]{:S(2)}) collective-permute-start(bf16[2,6,24,768]{3,2,1,0:T(8,128)(2,1)} %get-tuple-element.100), channel_id=1, source_target_pairs={{0,8},{2,10},{8,16},{10,18},{16,24},{18,26},{24,28},{26,30},{28,20... | collective-permute-start | bytes 1327112 | tf_op jit(solution)/shard_map/ppermute | solution.py:526
  276.9 13.9 %collective-permute-start.30 = (bf16[2,6,24,768]{3,2,1,0:T(8,128)(2,1)}, bf16[2,6,24,768]{3,2,1,0:T(8,128)(2,1)}, u32[]{:S(2)}, u32[]{:S(2)}) collective-permute-start(bf16[2,6,24,768]{3,2,1,0:T(8,128)(2,1)} %get-tuple-element.101), channel_id=1, source_target_pairs={{8,0},{10,2},{16,8},{18,10},{24,16},{26,18},{28,24},{30,26},{20,28... | collective-permute-start | bytes 1327112 | tf_op jit(solution)/shard_map/ppermute | solution.py:529
  283.5 18.3 %collective-permute-start.17 = (bf16[2,7,24,768]{3,2,1,0:T(8,128)(2,1)}, bf16[2,7,24,768]{3,2,1,0:T(8,128)(2,1)S(1)}, u32[]{:S(2)}, u32[]{:S(2)}) collective-permute-start(bf16[2,7,24,768]{3,2,1,0:T(8,128)(2,1)} %get-tuple-element.90), channel_id=1, source_target_pairs={{0,8},{2,10},{8,16},{10,18},{16,24},{18,26},{24,28},{26,30},{28,20... | collective-permute-start | bytes 1548296 | tf_op jit(solution)/shard_map/ppermute | solution.py:526
  284.6 17.2 %collective-permute-start.21 = (bf16[2,7,24,768]{3,2,1,0:T(8,128)(2,1)S(1)}, bf16[2,7,24,768]{3,2,1,0:T(8,128)(2,1)S(1)}, u32[]{:S(2)}, u32[]{:S(2)}) collective-permute-start(bf16[2,7,24,768]{3,2,1,0:T(8,128)(2,1)S(1)} %get-tuple-element.91), channel_id=1, source_target_pairs={{8,0},{10,2},{16,8},{18,10},{24,16},{26,18},{28,24},{30,26},{20,28... | collective-permute-start | bytes 1548296 | tf_op jit(solution)/shard_map/ppermute | solution.py:529
  292.4 18.8 %collective-permute-start.27 = (bf16[2,6,24,768]{3,2,1,0:T(8,128)(2,1)S(1)}, bf16[2,6,24,768]{3,2,1,0:T(8,128)(2,1)S(1)}, u32[]{:S(2)}, u32[]{:S(2)}) collective-permute-start(bf16[2,6,24,768]{3,2,1,0:T(8,128)(2,1)S(1)} %get-tuple-element.98), channel_id=1, source_target_pairs={{0,8},{2,10},{8,16},{10,18},{16,24},{18,26},{24,28},{26,30},{28,20... | collective-permute-start | bytes 1327112 | tf_op jit(solution)/shard_map/ppermute | solution.py:526
  293.6 17.6 %collective-permute-start.31 = (bf16[2,6,24,768]{3,2,1,0:T(8,128)(2,1)S(1)}, bf16[2,6,24,768]{3,2,1,0:T(8,128)(2,1)S(1)}, u32[]{:S(2)}, u32[]{:S(2)}) collective-permute-start(bf16[2,6,24,768]{3,2,1,0:T(8,128)(2,1)S(1)} %get-tuple-element.99), channel_id=1, source_target_pairs={{8,0},{10,2},{16,8},{18,10},{24,16},{26,18},{28,24},{30,26},{20,28... | collective-permute-start | bytes 1327112 | tf_op jit(solution)/shard_map/ppermute | solution.py:529
  303.2 15.0 %collective-permute-start.18 = (bf16[2,7,24,768]{3,2,1,0:T(8,128)(2,1)S(1)}, bf16[2,7,24,768]{3,2,1,0:T(8,128)(2,1)S(1)}, u32[]{:S(2)}, u32[]{:S(2)}) collective-permute-start(bf16[2,7,24,768]{3,2,1,0:T(8,128)(2,1)S(1)} %get-tuple-element.88), channel_id=1, source_target_pairs={{0,8},{2,10},{8,16},{10,18},{16,24},{18,26},{24,28},{26,30},{28,20... | collective-permute-start | bytes 1548296 | tf_op jit(solution)/shard_map/ppermute | solution.py:526
  304.5 13.7 %collective-permute-start.22 = (bf16[2,7,24,768]{3,2,1,0:T(8,128)(2,1)S(1)}, bf16[2,7,24,768]{3,2,1,0:T(8,128)(2,1)S(1)}, u32[]{:S(2)}, u32[]{:S(2)}) collective-permute-start(bf16[2,7,24,768]{3,2,1,0:T(8,128)(2,1)S(1)} %get-tuple-element.89), channel_id=1, source_target_pairs={{8,0},{10,2},{16,8},{18,10},{24,16},{26,18},{28,24},{30,26},{20,28... | collective-permute-start | bytes 1548296 | tf_op jit(solution)/shard_map/ppermute | solution.py:529
  332.1 23.8 %all-to-all-start = ((bf16[16,12,1536]{2,1,0:T(8,128)(2,1)}), bf16[16,12,1536]{2,1,0:T(8,128)(2,1)S(1)}, u32[]{:S(2)}, u32[]{:S(2)}) async-start(bf16[16,12,1536]{2,1,0:T(8,128)(2,1)} %select_select_fusion), calls=%async_computation | async-start | bytes 1572864 | tf_op jit(solution)/shard_map/all_to_all | solution.py:814
  (25 other events, 120.3 us)
Sparse Core Ops, SparseCore 0:
  11.5 127.4 all-gather.2
